TPU v7x, 512 devices: a whole 4x4x16 slice. The times are simulated.
512 devices in a mesh: fsdp: 32 (over y, z_hi, core), tp: 16 (over x, z_lo).
Axes of the slice: x: 4, y: 4, z: 16 (z_hi: 4, z_lo: 4; z = z_hi * 4 + z_lo), core: 2. Of those that a mesh axis runs over, the one named last changes fastest.
Arguments:
- tokens: bfloat16 [16384, 8192], P('fsdp', 'tp'), may hold values from -12 to 12
- fixed_query_weight: bfloat16 [8192, 8192], P('fsdp', 'tp'), may hold values from -0.0625 to 0.0625
- adapter_down_factor: bfloat16 [8, 8192], P(None, 'fsdp'), may hold values from -0.0625 to 0.0625
- adapter_up_factor: bfloat16 [8, 8192], P(None, 'tp'), may hold values from -0.125 to 0.125
- cotangent: bfloat16 [16384, 8192], P('fsdp', 'tp'), may hold values from -24 to 24
- importance: float32 [8192, 8192], P('fsdp', 'tp'), may hold values from 0.05 to 0.5
Outputs:
- projected: bfloat16 [16384, 8192], P('fsdp', 'tp')
- up_factor_gradient: float32 [8, 8192], P(None, 'tp')
- down_factor_gradient: float32 [8, 8192], P(None, 'fsdp')
- new_importance: float32 [8192, 8192], P('fsdp', 'tp')
All inputs are finite; a program needn't handle non-finite values.
Results may differ from a plain program's by a relative error of at most 0.0029.
Values may be sent and summed in bfloat16 or wider, within the bound.
A program may use at most 64 MiB of HBM per device.

v0:
```python
import jax
import jax.numpy as jnp
from jax import lax
from jax.sharding import PartitionSpec as P

adapter_scale = 2.0
decay_rate = 0.8


def local(
    tokens, fixed_query_weight, adapter_down_factor, adapter_up_factor, cotangent, importance
):
    own_rows = fixed_query_weight.shape[0]
    down_factor_columns = adapter_down_factor.T
    backward_product = lax.psum(
        jnp.dot(cotangent, adapter_up_factor.T, preferred_element_type=jnp.float32), "tp"
    )
    backward_product = backward_product.astype(jnp.bfloat16)
    weight_all, down_all = (
        lax.all_gather(fixed_query_weight, "fsdp", axis=0, tiled=True),
        lax.all_gather(down_factor_columns, "fsdp", axis=0, tiled=True),
    )
    piece = lax.all_gather(tokens, "tp", axis=1, tiled=True)
    projection_total = jnp.dot(piece, weight_all, preferred_element_type=jnp.float32)
    low_acc = jnp.dot(piece, down_all, preferred_element_type=jnp.float32)
    grad_part = jnp.dot(backward_product.T, piece, preferred_element_type=jnp.float32)
    gradient_product = grad_part
    rank_activation = low_acc.astype(jnp.bfloat16)
    projected = (
        projection_total
        + adapter_scale
        * jnp.dot(rank_activation, adapter_up_factor, preferred_element_type=jnp.float32)
    ).astype(jnp.bfloat16)
    up_factor_gradient = lax.psum(
        adapter_scale * jnp.dot(rank_activation.T, cotangent, preferred_element_type=jnp.float32),
        "fsdp",
    )
    gradient_product = adapter_scale * gradient_product
    grad_whole = lax.psum(gradient_product, "fsdp")
    down_factor_gradient = lax.dynamic_slice_in_dim(
        grad_whole, lax.axis_index("fsdp") * own_rows, own_rows, 1
    )
    merged_weight = fixed_query_weight.astype(jnp.float32) + adapter_scale * jnp.dot(
        down_factor_columns, adapter_up_factor, preferred_element_type=jnp.float32
    )
    importance_estimate = jnp.dot(
        down_factor_gradient.T,
        adapter_up_factor.astype(jnp.float32),
        precision=lax.Precision.HIGHEST,
    )
    importance_estimate = importance_estimate + jnp.dot(
        down_factor_columns.astype(jnp.float32), up_factor_gradient, precision=lax.Precision.HIGHEST
    )
    new_importance = decay_rate * importance + (1.0 - decay_rate) * jnp.abs(
        merged_weight * importance_estimate
    )
    return (projected, up_factor_gradient, down_factor_gradient, new_importance)


def solution(mesh):
    placed = (
        P("fsdp", "tp"),
        P("fsdp", "tp"),
        P(None, "fsdp"),
        P(None, "tp"),
        P("fsdp", "tp"),
        P("fsdp", "tp"),
    )
    return jax.shard_map(
        local,
        mesh=mesh,
        in_specs=placed,
        out_specs=(P("fsdp", "tp"), P(None, "tp"), P(None, "fsdp"), P("fsdp", "tp")),
        check_vma=False,
    )
```

profile of v0, /device:TPU:1, one launch (start us, length us, event | category | flops | bytes accessed | tf_op | source)
XLA Modules:
  0.0 712.6 jit_solution(11613898540451806211)
XLA Ops:
  7.2 0.0 copy-start
  7.2 0.0 copy-start.5
  7.2 0.0 all-gather.3.cloned.1.call-start
  7.2 0.7 all-gather.3.cloned.1.call-update
  7.9 0.0 all-reduce.2.cloned.1.call-start
  8.0 0.2 copy-done
  8.2 1.0 fusion.10
  9.2 80.6 %psum.22 = bf16[512,8]{1,0:T(8,128)(2,1)S(1)} all-reduce(f32[512,8]{1,0:T(8,128)S(1)} %fusion.10), channel_id=1, replica_groups=mesh['fsdp'=32,'tp'=16] {'tp'}, use_global_device_ids=true, to_apply=%region_1.0 | all-reduce | flops 4096 | bytes 24576 | tf_op jit(solution)/shard_map/psum | solution.py:15
  89.8 0.0 copy-start.3
  89.8 126.1 %all-gather.3.cloned.1.call-done = bf16[512,8192]{1,0:T(8,128)(2,1)} async-done(((bf16[512,512]{1,0:T(8,128)(2,1)}), bf16[512,8192]{1,0:T(8,128)(2,1)}) %all-gather.3.cloned.1.call-update) | async-done | bytes 8388624 | tf_op jit(solution)/shard_map/all_gather | solution.py:23
  215.9 5.3 convolution_multiply_fusion
  221.2 0.0 copy-start.1
  221.2 0.0 copy-start.2
  221.2 0.0 all-reduce.2.cloned.1.call-update
  221.2 0.0 all-gather.5.cloned.1.call-start
  221.3 0.7 all-gather.5.cloned.1.call-update
  222.0 0.0 copy-done.5
  222.0 53.6 %all_gather.11 = bf16[8192,8]{0,1:T(8,128)(2,1)S(1)} all-gather(bf16[256,8]{0,1:T(8,128)(2,1)S(1)} %bitcast.23), channel_id=1, replica_groups=mesh['fsdp'=32,'tp'=16] {'fsdp'}, dimensions={0}, use_global_device_ids=true | all-gather | bytes 135168 | tf_op jit(solution)/shard_map/all_gather | solution.py:21
  275.6 5.7 convolution_convert_fusion
  281.2 0.2 convolution_multiply_fusion.3
  281.4 161.0 %psum.21 = f32[8,512]{1,0:T(8,128)S(1)} all-reduce(f32[8,512]{1,0:T(8,128)S(1)} %convolution_multiply_fusion.3), channel_id=1, replica_groups=mesh['fsdp'=32,'tp'=16] {'fsdp'}, use_global_device_ids=true, to_apply=%region_0.0 | all-reduce | flops 4096 | bytes 32768 | tf_op jit(solution)/shard_map/psum | solution.py:34
  442.4 0.0 copy-start.4
  442.4 118.2 %all-reduce.2.cloned.1.call-done = f32[8,8192]{1,0:T(8,128)} async-done(((f32[8,8192]{1,0:T(8,128)}), f32[8,8192]{1,0:T(8,128)}) %all-reduce.2.cloned.1.call-update) | async-done | bytes 262160 | tf_op jit(solution)/shard_map/psum | solution.py:39
  560.6 0.7 constant_dynamic-slice_fusion
  561.3 0.0 copy-done.3
  561.3 0.0 copy-start.6
  561.3 0.4 fusion.11
  561.7 0.4 fusion.2
  562.1 0.0 copy-done.1
  562.1 0.0 copy-done.2
  562.1 1.1 fusion.7
  563.3 132.2 %all-gather.5.cloned.1.call-done = bf16[8192,512]{1,0:T(8,128)(2,1)} async-done(((bf16[256,512]{1,0:T(8,128)(2,1)}), bf16[8192,512]{1,0:T(8,128)(2,1)}) %all-gather.5.cloned.1.call-update) | async-done | bytes 8388624 | tf_op jit(solution)/shard_map/all_gather | solution.py:20
  695.4 9.4 %fusion.9 = f32[512,512]{1,0:T(8,128)S(1)} fusion(bf16[512,8192]{1,0:T(8,128)(2,1)} %all-gather.3.cloned.1.call-done, bf16[8192,512]{1,0:T(8,128)(2,1)} %all-gather.5.cloned.1.call-done), kind=kOutput, calls=%fused_computation.16 | convolution fusion | flops 4294967296 | bytes 17825792 | tf_op jit(solution)/shard_map/dot_general | solution.py:24
  704.9 0.0 copy-done.4
  704.9 0.0 copy-done.6
  704.9 1.1 fusion.1
Async XLA Ops:
  7.2 1.0 copy-start
  7.2 214.8 %copy-start.5 = (bf16[8,256]{1,0:T(8,128)(2,1)S(1)}, bf16[8,256]{1,0:T(8,128)(2,1)}, u32[]{:S(2)}) copy-start(bf16[8,256]{1,0:T(8,128)(2,1)} %param.8) | copy-start | bytes 12292
  7.2 208.7 %all-gather.3.cloned.1.call-start = ((), (), s32[]{:S(2)}) async-start(), calls=%async_computation | async-start | bytes 8912896 | tf_op jit(solution)/shard_map/all_gather | solution.py:23
  7.9 552.6 %all-reduce.2.cloned.1.call-start = ((), (), s32[]{:S(2)}) async-start(), calls=%async_computation.2 | async-start | bytes 524288 | tf_op jit(solution)/shard_map/psum | solution.py:39
  89.8 471.5 %copy-start.3 = (bf16[8,512]{1,0:T(8,128)(2,1)S(1)}, bf16[8,512]{1,0:T(8,128)(2,1)}, u32[]{:S(2)}) copy-start(bf16[8,512]{1,0:T(8,128)(2,1)} %param.9) | copy-start | bytes 24580
  221.2 340.9 %copy-start.1 = (bf16[256,512]{1,0:T(8,128)(2,1)S(1)}, bf16[256,512]{1,0:T(8,128)(2,1)}, u32[]{:S(2)}) copy-start(bf16[256,512]{1,0:T(8,128)(2,1)} %param.7) | copy-start | bytes 786436
  221.2 340.9 %copy-start.2 = (f32[256,512]{1,0:T(8,128)S(1)}, f32[256,512]{1,0:T(8,128)}, u32[]{:S(2)}) copy-start(f32[256,512]{1,0:T(8,128)} %param.11) | copy-start | bytes 1572868
  221.2 474.2 %all-gather.5.cloned.1.call-start = ((), (), s32[]{:S(2)}) async-start(), calls=%async_computation.1 | async-start | bytes 8650752 | tf_op jit(solution)/shard_map/all_gather | solution.py:20
  442.4 262.5 %copy-start.4 = (f32[8,512]{1,0:T(8,128)}, f32[8,512]{1,0:T(8,128)S(1)}, u32[]{:S(2)}) copy-start(f32[8,512]{1,0:T(8,128)S(1)} %psum.21) | copy-start | bytes 49156
  561.3 143.6 %copy-start.6 = (f32[8,256]{1,0:T(8,128)}, f32[8,256]{1,0:T(8,128)S(1)}, u32[]{:S(2)}) copy-start(f32[8,256]{1,0:T(8,128)S(1)} %constant_dynamic-slice_fusion) | copy-start | bytes 24580
Sparse Core Ops, SparseCore 0:
  10.1 205.7 all-gather.2
  221.3 339.1 all-reduce.1
  564.2 131.2 all-gather.4
where the time goes:
time: 713 us
  waiting for transfers between devices  378 us (53%)
  blocking collectives  295 us (41%)
  matrix products  24.7 us (3%)
  between operations  13.9 us (2%)
    psum x1, blocking collectives, local(): lax.psum(adapter_scale * jnp.dot(rank_activation.T, cotangent, preferred_...  161 us
    all_gather x1, waiting for transfers between devices, local(): lax.all_gather(fixed_query_weight, 'fsdp', axis=0, tiled=True)  132 us
    all_gather x1, waiting for transfers between devices, local(): piece = lax.all_gather(tokens, 'tp', axis=1, tiled=True)  126 us
    psum x1, waiting for transfers between devices, local(): grad_whole = lax.psum(gradient_product, 'fsdp')  118 us
    psum x1, blocking collectives, local(): lax.psum(jnp.dot(cotangent, adapter_up_factor.T, preferred_element_type=j...  80.6 us
    all_gather x1, blocking collectives, local(): lax.all_gather(down_factor_columns, 'fsdp', axis=0, tiled=True)  53.6 us
  transfers between devices with their start and end apart: 3, of which 3 were waited for; matrix products, arithmetic and copies ran while one was open for 1% of the time, Pallas kernels for 0%

commit v1 on v0

v1 whole, which is shorter than its diff:
```python
import jax
import jax.numpy as jnp
from jax import lax
from jax.experimental import pallas as pl
from jax.experimental.pallas import tpu as pltpu
from jax.sharding import PartitionSpec as P

adapter_scale = 2.0
decay_rate = 0.8
MESH = pl.DeviceIdType.MESH
WEIGHT_START = 2


def dot(a, b, dims, precision=None):
    return lax.dot_general(
        a, b, (dims, ((), ())), preferred_element_type=jnp.float32, precision=precision
    )


def kernel(
    tok_in, w_in, down, up, cot_in, imp_in,
    proj_out, upg_out, dng_out, newimp_out,
    T, W, acc, proj, cot, imp, newimp, upg, dng, down_t, dtot,
    arx, arz, arc, ary, arh,
    load_sem, store_sem,
    tx_s, tx_r, txh_s, txh_r, tz_s, tz_r,
    wz_s, wz_r, wzh_s, wzh_r, wy_s, wy_r, wyh_s, wyh_r, wc_s, wc_r,
    arx_s, arx_r, arz_s, arz_r, arc_s, arc_r, ary_s, ary_r, arh_s, arh_r,
    dt_s, dt_r, dg_s, dg_r,
):
    f = lax.axis_index("fsdp")
    t = lax.axis_index("tp")
    chip = f // 2
    c = f % 2
    y, zh = chip // 4, chip % 4
    x, zl = t // 4, t % 4

    def dev(y=y, zh=zh, c=c, x=x, zl=zl):
        return {"fsdp": (y * 4 + zh) * 2 + c, "tp": x * 4 + zl}

    def ring(i, d):
        return (i + d + 4) % 4

    x_next, x_prev = dev(x=ring(x, 1)), dev(x=ring(x, -1))
    y_next, y_prev = dev(y=ring(y, 1)), dev(y=ring(y, -1))
    h_next, h_prev = dev(zh=ring(zh, 1)), dev(zh=ring(zh, -1))
    l_next, l_prev = dev(zl=ring(zl, 1)), dev(zl=ring(zl, -1))
    sibling = dev(c=1 - c)
    off_diagonal = chip != t

    def mirror(core):
        return {"fsdp": t * 2 + core, "tp": chip}

    def remote(src, dst, send, recv, to):
        return pltpu.make_async_remote_copy(
            src_ref=src, dst_ref=dst, send_sem=send, recv_sem=recv, device_id=to, device_id_type=MESH
        )

    loads = [
        pltpu.make_async_copy(src, dst, load_sem.at[i])
        for i, (src, dst) in enumerate(
            [
                (tok_in, T.at[x, zl]),
                (w_in, W.at[y, zh, c]),
                (cot_in, cot),
                (imp_in, imp),
            ]
        )
    ]
    for load in loads:
        load.start()

    barrier = pltpu.get_barrier_semaphore()
    for r in (1, 2, 3):
        for partner in (dev(x=ring(x, r)), dev(y=ring(y, r)), dev(zh=ring(zh, r)), dev(zl=ring(zl, r))):
            pl.semaphore_signal(barrier, inc=1, device_id=partner, device_id_type=MESH)
    pl.semaphore_signal(barrier, inc=1, device_id=sibling, device_id_type=MESH)

    @pl.when(off_diagonal)
    def _():
        for core in (0, 1):
            pl.semaphore_signal(barrier, inc=1, device_id=mirror(core), device_id_type=MESH)

    for load in loads[:2]:
        load.wait()
    down_f32 = down[...].astype(jnp.float32)
    dtot[2] = down_f32
    pl.semaphore_wait(barrier, jnp.where(off_diagonal, 15, 13))

    sends = []

    def go(copy):
        copy.start()
        sends.append(copy)
        return copy

    down_away = remote(dtot.at[2], down_t.at[c], dt_s.at[0], dt_r.at[c], sibling)
    down_mirror = [
        remote(dtot.at[2], down_t.at[c], dt_s.at[1 + core], dt_r.at[c], mirror(core)) for core in (0, 1)
    ]

    @pl.when(jnp.logical_not(off_diagonal))
    def _():
        down_t[c] = down_f32
        down_away.start()

    @pl.when(off_diagonal)
    def _():
        for copy in down_mirror:
            copy.start()

    unit = [
        zl,
        jnp.where(zl == 0, 1, jnp.where(zl == 1, 0, jnp.where(zl == 2, 1, 2))),
        jnp.where(zl == 0, 2, jnp.where(zl == 1, 2, jnp.where(zl == 2, 3, 1))),
        jnp.where(zl < 2, 3, 0),
    ]
    wunit = [zh, ring(zh, -1), ring(zh, 1), ring(zh, 2)]

    def send_x(j):
        for side, to in enumerate((x_next, x_prev)):
            go(remote(T.at[x, unit[j]], T.at[x, unit[j]], tx_s.at[side, j], tx_r.at[side, j], to))

    z_forwards = []

    def send_z(j):
        block = T.at[x, unit[j]]
        if j == 0:
            cases = ((zl < 3, l_next, 0), (zl > 0, l_prev, 1))
        else:
            cases = (
                (jnp.logical_and(unit[j] < zl, zl < 3), l_next, 0),
                (jnp.logical_and(unit[j] > zl, zl > 0), l_prev, 1),
            )
        for cond, to, side in cases:
            copy = remote(block, block, tz_s.at[side, j], tz_r.at[unit[j]], to)
            z_forwards.append((cond, copy))

            @pl.when(cond)
            def _(copy=copy):
                copy.start()

    def recv(dst, sem):
        remote(dst, dst, sem, sem, sibling).wait_recv()

    def recv_z(j):
        recv(T.at[x, unit[j]], tz_r.at[unit[j]])
        send_z(j)
        send_x(j)

    half = 256

    def recv_x(j):
        left, right = ring(x, -1), ring(x, 1)
        recv(T.at[left, unit[j]], tx_r.at[0, j])
        block = T.at[left, unit[j], pl.ds(0, half)]
        go(remote(block, block, txh_s.at[0, j], txh_r.at[0, j], x_next))
        recv(T.at[right, unit[j]], tx_r.at[1, j])
        block = T.at[right, unit[j], pl.ds(half, half)]
        go(remote(block, block, txh_s.at[1, j], txh_r.at[1, j], x_prev))

    def recv_xh(j):
        far = ring(x, 2)
        recv(T.at[far, unit[j], pl.ds(0, half)], txh_r.at[0, j])
        recv(T.at[far, unit[j], pl.ds(half, half)], txh_r.at[1, j])

    quarter = 128

    def send_c(u, r):
        block = W.at[ring(y, r), wunit[u], c]
        go(remote(block, block, wc_s.at[u, r % 4], wc_r.at[u, r % 4], sibling))

    def send_y(u):
        block = W.at[y, wunit[u], c]
        for side, to in enumerate((y_next, y_prev)):
            go(remote(block, block, wy_s.at[side, u], wy_r.at[side, u], to))
        send_c(u, 0)

    def recv_y(u):
        left, right = ring(y, -1), ring(y, 1)
        recv(W.at[left, wunit[u], c], wy_r.at[0, u])
        block = W.at[left, wunit[u], c, pl.ds(0, quarter)]
        go(remote(block, block, wyh_s.at[0, u], wyh_r.at[0, u], y_next))
        send_c(u, -1)
        recv(W.at[right, wunit[u], c], wy_r.at[1, u])
        block = W.at[right, wunit[u], c, pl.ds(quarter, quarter)]
        go(remote(block, block, wyh_s.at[1, u], wyh_r.at[1, u], y_prev))
        send_c(u, 1)

    def recv_yh(u):
        far = ring(y, 2)
        recv(W.at[far, wunit[u], c, pl.ds(0, quarter)], wyh_r.at[0, u])
        recv(W.at[far, wunit[u], c, pl.ds(quarter, quarter)], wyh_r.at[1, u])
        send_c(u, 2)

    def recv_c(u):
        for r in range(4):
            recv(W.at[ring(y, r), wunit[u], 1 - c], wc_r.at[u, r])

    def send_wz():
        block = W.at[y, zh, c]
        for side, to in enumerate((h_next, h_prev)):
            go(remote(block, block, wz_s.at[side], wz_r.at[side], to))

    def recv_wz():
        left, right = wunit[1], wunit[2]
        recv(W.at[y, left, c], wz_r.at[0])
        block = W.at[y, left, c, pl.ds(0, quarter)]
        go(remote(block, block, wzh_s.at[0], wzh_r.at[0], h_next))
        send_y(1)
        recv(W.at[y, right, c], wz_r.at[1])
        block = W.at[y, right, c, pl.ds(quarter, quarter)]
        go(remote(block, block, wzh_s.at[1], wzh_r.at[1], h_prev))
        send_y(2)

    def recv_wzh():
        recv(W.at[y, wunit[3], c, pl.ds(0, quarter)], wzh_r.at[0])
        recv(W.at[y, wunit[3], c, pl.ds(quarter, quarter)], wzh_r.at[1])
        send_y(3)

    def sum_send(buf, me, s, r, to):
        for d in range(1, len(to) + 1):
            go(remote(buf.at[me], buf.at[me], s.at[d - 1], r.at[me], to[d - 1]))

    def sum_recv(buf, me, r, n):
        for d in range(1, n):
            other = (me + d) % n
            recv(buf.at[other], r.at[other])
        total = buf[0] + buf[1]
        for i in range(2, n):
            total = total + buf[i]
        return total

    send_x(0)
    send_z(0)
    send_y(0)
    if WEIGHT_START == 0:
        send_wz()
    for load in loads[2:]:
        load.wait()

    @pl.when(off_diagonal)
    def _():
        recv(down_t.at[c], dt_r.at[c])

    recv(down_t.at[1 - c], dt_r.at[1 - c])
    tok = T[x, zl]
    down_columns = jnp.concatenate([down_t[0], down_t[1]], axis=1).astype(jnp.bfloat16)
    arx[x, 0:8] = dot(down_columns, tok, ((1,), (1,)))
    arx[x, 8:16] = dot(up[...], cot[...], ((1,), (1,)))
    sum_send(arx, x, arx_s, arx_r, [dev(x=ring(x, d)) for d in (1, 2, 3)])

    recv_y(0)
    recv_z(1)
    recv_x(0)

    arz[zl] = sum_recv(arx, x, arx_r, 4)
    sum_send(arz, zl, arz_s, arz_r, [dev(zl=ring(zl, d)) for d in (1, 2, 3)])
    if WEIGHT_START == 1:
        send_wz()
    recv_z(2)
    if WEIGHT_START == 2:
        send_wz()
    recv_yh(0)

    both = sum_recv(arz, zl, arz_r, 4)
    low, back = both[0:8].astype(jnp.bfloat16), both[8:16].astype(jnp.bfloat16)
    arc[c, 0:8] = adapter_scale * dot(low, cot[...], ((1,), (0,)))
    arc[c, 8:16] = adapter_scale * dot(back, T[x, zl], ((1,), (0,)))
    sum_send(arc, c, arc_s, arc_r, [sibling])
    acc[...] = adapter_scale * dot(low, up[...], ((0,), (0,)))

    recv_x(1)
    ary[y] = sum_recv(arc, c, arc_r, 2)
    sum_send(ary, y, ary_s, ary_r, [dev(y=ring(y, d)) for d in (1, 2, 3)])
    recv_z(3)
    if WEIGHT_START == 3:
        send_wz()
    recv_xh(0)
    recv_c(0)

    def products(stage):
        for u in range(4):
            here = 0
            for j in range(4):
                here = here + jnp.where(unit[j] == wunit[u], j, 0)

            @pl.when(jnp.maximum(here, u) == stage)
            def _(u=u):
                @pl.loop(0, 4)
                def _(i):
                    weights = W[i, wunit[u]].reshape(512, 512)
                    for r in range(2):
                        rows = pl.ds(r * 256, 256)
                        acc[rows] += dot(T[i, wunit[u], rows], weights, ((1,), (0,)))

    products(0)
    arh[zh] = sum_recv(ary, y, ary_r, 4)
    sum_send(arh, zh, arh_s, arh_r, [dev(zh=ring(zh, d)) for d in (1, 2, 3)])
    recv_x(2)
    recv_wz()
    recv_xh(1)

    grads = sum_recv(arh, zh, arh_r, 4)
    upg[...] = grads[0:8]
    dtot[0] = grads[8:16, 0:256]
    dtot[1] = grads[8:16, 256:512]
    gradient_mirror = remote(dtot.at[c], dng, dg_s, dg_r, mirror(c))

    @pl.when(off_diagonal)
    def _():
        gradient_mirror.start()

    @pl.when(jnp.logical_not(off_diagonal))
    def _():
        dng[...] = dtot[c]

    recv_y(1)
    recv_y(2)
    recv_wzh()
    recv_x(3)

    @pl.when(off_diagonal)
    def _():
        gradient_mirror.wait_recv()

    stores = [
        pltpu.make_async_copy(src, dst, store_sem.at[i])
        for i, (src, dst) in enumerate(
            [(upg, upg_out), (dng, dng_out), (newimp, newimp_out), (proj, proj_out)]
        )
    ]
    stores[0].start()
    stores[1].start()
    highest = lax.Precision.HIGHEST
    own_down = down[...]
    estimate = dot(dng[...], up[...].astype(jnp.float32), ((0,), (0,)), highest)
    estimate = estimate + dot(own_down.astype(jnp.float32), upg[...], ((0,), (0,)), highest)
    merged = W[y, zh, c].astype(jnp.float32) + adapter_scale * dot(own_down, up[...], ((0,), (0,)))
    newimp[...] = decay_rate * imp[...] + (1.0 - decay_rate) * jnp.abs(merged * estimate)
    stores[2].start()

    recv_yh(1)
    recv_yh(2)
    recv_c(1)
    products(1)
    recv_y(3)
    recv_xh(2)
    recv_yh(3)
    recv_c(2)
    products(2)
    recv_c(3)
    recv_xh(3)
    products(3)
    proj[...] = acc[...].astype(jnp.bfloat16)
    stores[3].start()

    for copy in sends:
        copy.wait_send()
    for cond, copy in z_forwards:

        @pl.when(cond)
        def _(copy=copy):
            copy.wait_send()

    @pl.when(jnp.logical_not(off_diagonal))
    def _():
        down_away.wait_send()

    @pl.when(off_diagonal)
    def _():
        for copy in down_mirror:
            copy.wait_send()
        gradient_mirror.wait_send()

    for store in stores:
        store.wait()


def local(tokens, weight, down, up, cotangent, importance):
    bf16, f32 = jnp.bfloat16, jnp.float32
    dma = pltpu.SemaphoreType.DMA
    return pl.pallas_call(
        kernel,
        out_shape=(
            jax.ShapeDtypeStruct((512, 512), bf16),
            jax.ShapeDtypeStruct((8, 512), f32),
            jax.ShapeDtypeStruct((8, 256), f32),
            jax.ShapeDtypeStruct((256, 512), f32),
        ),
        in_specs=[
            pl.BlockSpec(memory_space=pltpu.VMEM if i in (2, 3) else pl.ANY) for i in range(6)
        ],
        out_specs=[pl.BlockSpec(memory_space=pl.ANY)] * 4,
        scratch_shapes=[
            pltpu.VMEM((4, 4, 512, 512), bf16),
            pltpu.VMEM((4, 4, 2, 256, 512), bf16),
            pltpu.VMEM((512, 512), f32),
            pltpu.VMEM((512, 512), bf16),
            pltpu.VMEM((512, 512), bf16),
            pltpu.VMEM((256, 512), f32),
            pltpu.VMEM((256, 512), f32),
            pltpu.VMEM((8, 512), f32),
            pltpu.VMEM((8, 256), f32),
            pltpu.VMEM((2, 8, 256), f32),
            pltpu.VMEM((3, 8, 256), f32),
            pltpu.VMEM((4, 16, 512), f32),
            pltpu.VMEM((4, 16, 512), f32),
            pltpu.VMEM((2, 16, 512), f32),
            pltpu.VMEM((4, 16, 512), f32),
            pltpu.VMEM((4, 16, 512), f32),
            dma((4,)), dma((4,)),
            dma((2, 4)), dma((2, 4)), dma((2, 4)), dma((2, 4)), dma((2, 4)), dma((4,)),
            dma((2,)), dma((2,)), dma((2,)), dma((2,)),
            dma((2, 4)), dma((2, 4)), dma((2, 4)), dma((2, 4)), dma((4, 4)), dma((4, 4)),
            dma((3,)), dma((4,)), dma((3,)), dma((4,)), dma((1,)), dma((2,)),
            dma((3,)), dma((4,)), dma((3,)), dma((4,)),
            dma((3,)), dma((2,)), dma, dma,
        ],
        compiler_params=pltpu.CompilerParams(
            collective_id=0, has_side_effects=True, vmem_limit_bytes=48 * 2**20
        ),
    )(tokens, weight, down, up, cotangent, importance)


def solution(mesh):
    placed = (
        P("fsdp", "tp"),
        P("fsdp", "tp"),
        P(None, "fsdp"),
        P(None, "tp"),
        P("fsdp", "tp"),
        P("fsdp", "tp"),
    )
    return jax.shard_map(
        local,
        mesh=mesh,
        in_specs=placed,
        out_specs=(P("fsdp", "tp"), P(None, "tp"), P(None, "fsdp"), P("fsdp", "tp")),
        check_vma=False,
    )
```

time: 713 us -> 142 us (0.20)
  waiting for transfers between devices: 378 us -> 0 us
  blocking collectives: 295 us -> 0 us
  Pallas kernels: 0 us -> 132 us
  matrix products: 24.7 us -> 0 us
  between operations: 13.9 us -> 0.66 us
  local copies, waits for them, and re-layouts: 0.97 us -> 8.24 us
    all_gather x2 -> x0, waiting for transfers between devices: 258 us -> none  [the longest x1 132 us: local(): lax.all_gather(fixed_query_weight, 'fsdp', axis=0, tiled=True)]
    psum x2 -> x0, blocking collectives: 242 us -> none  [the longest x1 161 us: local(): lax.psum(adapter_scale * jnp.dot(rank_activation.T, cotangent, preferred_...]
    pallas_call x0 -> x1, Pallas kernels: none -> 132 us  [local(): pl.pallas_call(kernel, out_shape=(jax.ShapeDtypeStruct((512, 512), bf16),...]
    psum x1 -> x0, waiting for transfers between devices: 118 us -> none  [local(): grad_whole = lax.psum(gradient_product, 'fsdp')]
    all_gather x1 -> x0, blocking collectives: 53.6 us -> none  [local(): lax.all_gather(down_factor_columns, 'fsdp', axis=0, tiled=True)]
    dot_general x9 -> x0, matrix products: 24.7 us -> none  [the longest x1 9.44 us: local(): jnp.dot(piece, weight_all, preferred_element_type=jnp.float32)]
    unnamed x14 -> x16, local copies, waits for them, and re-layouts: 0.27 us -> 8.24 us
  transfers between devices with their start and end apart: 3 -> 0, of which waited for: 3 -> 0; matrix products, arithmetic and copies ran while one was open for 1% -> 0% of each run, Pallas kernels for 0% -> 0%
where the time goes in v1:
time: 142 us; the launch traced here: 141 us
  Pallas kernels  132 us (93%)
  local copies, waits for them, and re-layouts  8.24 us (6%)
    pallas_call x1, Pallas kernels, local(): pl.pallas_call(kernel, out_shape=(jax.ShapeDtypeStruct((512, 512), bf16),...  132 us
    unnamed x16, local copies, waits for them, and re-layouts  8.24 us

profile of v1, /device:TPU:1, one launch (start us, length us, event | category | flops | bytes accessed | tf_op | source)
XLA Modules:
  0.0 141.2 jit_solution(17195586366882559911)
XLA Ops:
  0.6 0.0 copy-start
  0.6 1.0 copy-done
  1.7 0.0 copy-start.1
  1.7 1.0 copy-done.1
  2.7 0.0 copy-start.2
  2.7 1.0 copy-done.2
  3.8 0.0 copy-start.3
  3.8 0.9 copy-done.3
  4.7 0.0 copy-start.4
  4.7 0.7 copy-done.4
  5.4 0.0 copy-start.5
  5.4 0.7 copy-done.5
  6.1 132.3 %shard_map.93 = (bf16[512,512]{1,0:T(8,128)(2,1)S(1)}, f32[8,512]{1,0:T(8,128)S(1)}, f32[8,256]{1,0:T(8,128)S(1)}, f32[256,512]{1,0:T(8,128)S(1)}) custom-call(bf16[512,512]{1,0:T(8,128)(2,1)S(1)} %copy-done, bf16[256,512]{1,0:T(8,128)(2,1)S(1)} %copy-done.3, bf16[8,256]{1,0:T(8,128)(2,1)S(1)} %copy-done.5, bf16[8,512]{1,0:T(8,128)(2,1)S(1)} %copy-done.4, ...), custom_call_target="tpu_custom_call" | custom-call | tf_op jit(solution)/shard_map/pallas_call | solution.py:383
  138.4 0.8 copy.14
  139.2 0.6 copy.15
  139.8 0.6 copy.16
  140.4 0.8 copy.17
Async XLA Ops:
  0.6 1.0 copy-start
  1.7 1.0 copy-start.1
  2.7 1.0 copy-start.2
  3.8 0.9 copy-start.3
  4.7 0.7 copy-start.4
  5.4 0.7 copy-start.5

commit v2 on v1

v2 whole, which is shorter than its diff:
```python
import jax
import jax.numpy as jnp
from jax import lax
from jax.experimental import pallas as pl
from jax.experimental.pallas import tpu as pltpu
from jax.sharding import PartitionSpec as P

adapter_scale = 2.0
decay_rate = 0.8
MESH = pl.DeviceIdType.MESH


def dot(a, b, dims, precision=None):
    return lax.dot_general(
        a, b, (dims, ((), ())), preferred_element_type=jnp.float32, precision=precision
    )


def kernel(
    tok_in, w_in, down, up, cot_in, imp_in,
    proj_out, upg_out, dng_out, newimp_out,
    T, W, acc, proj, cot, imp, newimp, upg, dng, down_t, dtot,
    arx, arz, arc, ary, arh,
    load_sem, store_sem,
    tx_s, tx_r, txh_s, txh_r, tz_s, tz_r,
    wz_s, wz_r, wzh_s, wzh_r, wy_s, wy_r, wyh_s, wyh_r, wc_s, wc_r,
    arx_s, arx_r, arz_s, arz_r, arc_s, arc_r, ary_s, ary_r, arh_s, arh_r,
    dt_s, dt_r, dg_s, dg_r,
):
    f = lax.axis_index("fsdp")
    t = lax.axis_index("tp")
    chip = f // 2
    c = f % 2
    y, zh = chip // 4, chip % 4
    x, zl = t // 4, t % 4

    def dev(y=y, zh=zh, c=c, x=x, zl=zl):
        return {"fsdp": (y * 4 + zh) * 2 + c, "tp": x * 4 + zl}

    def ring(i, d):
        return (i + d + 4) % 4

    x_next, x_prev = dev(x=ring(x, 1)), dev(x=ring(x, -1))
    y_next, y_prev = dev(y=ring(y, 1)), dev(y=ring(y, -1))
    h_next, h_prev = dev(zh=ring(zh, 1)), dev(zh=ring(zh, -1))
    l_next, l_prev = dev(zl=ring(zl, 1)), dev(zl=ring(zl, -1))
    sibling = dev(c=1 - c)
    off_diagonal = chip != t

    def mirror(core):
        return {"fsdp": t * 2 + core, "tp": chip}

    def remote(src, dst, send, recv, to):
        return pltpu.make_async_remote_copy(
            src_ref=src, dst_ref=dst, send_sem=send, recv_sem=recv, device_id=to, device_id_type=MESH
        )

    loads = [
        pltpu.make_async_copy(src, dst, load_sem.at[i])
        for i, (src, dst) in enumerate(
            [
                (tok_in, T.at[x, zl]),
                (w_in, W.at[y, zh, c]),
                (cot_in, cot),
                (imp_in, imp),
            ]
        )
    ]
    for load in loads:
        load.start()

    barrier = pltpu.get_barrier_semaphore()
    for r in (1, 2, 3):
        for partner in (dev(x=ring(x, r)), dev(y=ring(y, r)), dev(zh=ring(zh, r)), dev(zl=ring(zl, r))):
            pl.semaphore_signal(barrier, inc=1, device_id=partner, device_id_type=MESH)
    pl.semaphore_signal(barrier, inc=1, device_id=sibling, device_id_type=MESH)

    @pl.when(off_diagonal)
    def _():
        for core in (0, 1):
            pl.semaphore_signal(barrier, inc=1, device_id=mirror(core), device_id_type=MESH)

    for load in loads[:2]:
        load.wait()
    down_f32 = down[...].astype(jnp.float32)
    dtot[2] = down_f32
    pl.semaphore_wait(barrier, jnp.where(off_diagonal, 15, 13))

    sends = []

    def go(copy):
        copy.start()
        sends.append(copy)
        return copy

    down_away = remote(dtot.at[2], down_t.at[c], dt_s.at[0], dt_r.at[c], sibling)
    down_mirror = [
        remote(dtot.at[2], down_t.at[c], dt_s.at[1 + core], dt_r.at[c], mirror(core)) for core in (0, 1)
    ]

    @pl.when(jnp.logical_not(off_diagonal))
    def _():
        down_t[c] = down_f32
        down_away.start()

    @pl.when(off_diagonal)
    def _():
        for copy in down_mirror:
            copy.start()

    unit = [
        zl,
        jnp.where(zl == 0, 1, jnp.where(zl == 1, 0, jnp.where(zl == 2, 1, 2))),
        jnp.where(zl == 0, 2, jnp.where(zl == 1, 2, jnp.where(zl == 2, 3, 1))),
        jnp.where(zl < 2, 3, 0),
    ]
    wunit = [zh, ring(zh, -1), ring(zh, 1), ring(zh, 2)]

    half, quarter = 256, 128

    def rows(h, size):
        return pl.ds(h * size, size)

    def recv(dst, sem):
        remote(dst, dst, sem, sem, sibling).wait_recv()

    def send_x(j, h):
        block = T.at[x, unit[j], rows(h, half)]
        for side, to in enumerate((x_next, x_prev)):
            go(remote(block, block, tx_s.at[side, j, h], tx_r.at[side, j, h], to))

    def send_x0(k):
        for side, to in enumerate((x_next, x_prev)):
            h = k if side == 0 else 1 - k
            block = T.at[x, zl, rows(h, half)]
            go(remote(block, block, tx_s.at[side, 0, h], tx_r.at[side, 0, h], to))

    z_forwards = []

    def send_z(j, h):
        block = T.at[x, unit[j], rows(h, half)]
        if j == 0:
            cases = ((zl < 3, l_next, 0), (zl > 0, l_prev, 1))
        else:
            cases = (
                (jnp.logical_and(unit[j] < zl, zl < 3), l_next, 0),
                (jnp.logical_and(unit[j] > zl, zl > 0), l_prev, 1),
            )
        for cond, to, side in cases:
            copy = remote(block, block, tz_s.at[side, j, h], tz_r.at[unit[j], h], to)
            z_forwards.append((cond, copy))

            @pl.when(cond)
            def _(copy=copy):
                copy.start()

    def recv_z(j, h):
        recv(T.at[x, unit[j], rows(h, half)], tz_r.at[unit[j], h])
        send_z(j, h)
        send_x(j, h)

    def forward_x(j, h):
        near, to = (ring(x, -1), x_next) if h == 0 else (ring(x, 1), x_prev)
        block = T.at[near, unit[j], rows(h, half)]
        recv(block, tx_r.at[h, j, h])
        go(remote(block, block, txh_s.at[h, j], txh_r.at[h, j], to))

    def rest_x(j):
        recv(T.at[ring(x, -1), unit[j], rows(1, half)], tx_r.at[0, j, 1])
        recv(T.at[ring(x, 1), unit[j], rows(0, half)], tx_r.at[1, j, 0])

    def far_x(j):
        for h in (0, 1):
            recv(T.at[ring(x, 2), unit[j], rows(h, half)], txh_r.at[h, j])

    def send_c(u, r):
        block = W.at[ring(y, r), wunit[u], c]
        go(remote(block, block, wc_s.at[u, r % 4], wc_r.at[u, r % 4], sibling))

    def send_y(u, h):
        block = W.at[y, wunit[u], c, rows(h, quarter)]
        for side, to in enumerate((y_next, y_prev)):
            go(remote(block, block, wy_s.at[side, u, h], wy_r.at[side, u, h], to))

    def forward_y(u, h):
        near, to = (ring(y, -1), y_next) if h == 0 else (ring(y, 1), y_prev)
        block = W.at[near, wunit[u], c, rows(h, quarter)]
        recv(block, wy_r.at[h, u, h])
        go(remote(block, block, wyh_s.at[h, u], wyh_r.at[h, u], to))

    def rest_y(u):
        recv(W.at[ring(y, -1), wunit[u], c, rows(1, quarter)], wy_r.at[0, u, 1])
        send_c(u, -1)
        recv(W.at[ring(y, 1), wunit[u], c, rows(0, quarter)], wy_r.at[1, u, 0])
        send_c(u, 1)

    def far_y(u):
        for h in (0, 1):
            recv(W.at[ring(y, 2), wunit[u], c, rows(h, quarter)], wyh_r.at[h, u])
        send_c(u, 2)

    def recv_c(u):
        for r in range(4):
            recv(W.at[ring(y, r), wunit[u], 1 - c], wc_r.at[u, r])

    def send_wz(k):
        for side, to in enumerate((h_next, h_prev)):
            h = k if side == 0 else 1 - k
            block = W.at[y, zh, c, rows(h, quarter)]
            go(remote(block, block, wz_s.at[side, h], wz_r.at[side, h], to))

    def forward_wz(h):
        near, to = (wunit[1], h_next) if h == 0 else (wunit[2], h_prev)
        block = W.at[y, near, c, rows(h, quarter)]
        recv(block, wz_r.at[h, h])
        go(remote(block, block, wzh_s.at[h], wzh_r.at[h], to))
        send_y(1 + h, h)

    def rest_wz():
        recv(W.at[y, wunit[1], c, rows(1, quarter)], wz_r.at[0, 1])
        send_y(1, 1)
        send_c(1, 0)
        recv(W.at[y, wunit[2], c, rows(0, quarter)], wz_r.at[1, 0])
        send_y(2, 0)
        send_c(2, 0)

    def far_wz():
        for h in (0, 1):
            recv(W.at[y, wunit[3], c, rows(h, quarter)], wzh_r.at[h])
            send_y(3, h)
        send_c(3, 0)

    def sum_send(buf, me, s, r, to):
        for d in range(1, len(to) + 1):
            go(remote(buf.at[me], buf.at[me], s.at[d - 1], r.at[me], to[d - 1]))

    def sum_recv(buf, me, r, n):
        for d in range(1, n):
            other = (me + d) % n
            recv(buf.at[other], r.at[other])
        total = buf[0] + buf[1]
        for i in range(2, n):
            total = total + buf[i]
        return total

    send_x0(0)
    for h in (0, 1):
        send_z(0, h)
        send_y(0, h)
    send_c(0, 0)
    for load in loads[2:]:
        load.wait()

    @pl.when(off_diagonal)
    def _():
        recv(down_t.at[c], dt_r.at[c])

    recv(down_t.at[1 - c], dt_r.at[1 - c])
    down_columns = jnp.concatenate([down_t[0], down_t[1]], axis=1).astype(jnp.bfloat16)
    arx[x, 0:8] = dot(down_columns, T[x, zl], ((1,), (1,)))
    arx[x, 8:16] = dot(up[...], cot[...], ((1,), (1,)))
    sum_send(arx, x, arx_s, arx_r, [dev(x=ring(x, d)) for d in (1, 2, 3)])
    send_x0(1)

    def sum_low():
        arz[zl] = sum_recv(arx, x, arx_r, 4)
        sum_send(arz, zl, arz_s, arz_r, [dev(zl=ring(zl, d)) for d in (1, 2, 3)])

    def factor_terms():
        both = sum_recv(arz, zl, arz_r, 4)
        low, back = both[0:8].astype(jnp.bfloat16), both[8:16].astype(jnp.bfloat16)
        arc[c, 0:8] = adapter_scale * dot(low, cot[...], ((1,), (0,)))
        arc[c, 8:16] = adapter_scale * dot(back, T[x, zl], ((1,), (0,)))
        sum_send(arc, c, arc_s, arc_r, [sibling])
        acc[...] = adapter_scale * dot(low, up[...], ((0,), (0,)))

    def sum_cores():
        ary[y] = sum_recv(arc, c, arc_r, 2)
        sum_send(ary, y, ary_s, ary_r, [dev(y=ring(y, d)) for d in (1, 2, 3)])

    def sum_y():
        arh[zh] = sum_recv(ary, y, ary_r, 4)
        sum_send(arh, zh, arh_s, arh_r, [dev(zh=ring(zh, d)) for d in (1, 2, 3)])

    def gradient_copy():
        return remote(dtot.at[c], dng, dg_s, dg_r, mirror(c))

    def sum_gradients():
        grads = sum_recv(arh, zh, arh_r, 4)
        upg[...] = grads[0:8]
        dtot[0] = grads[8:16, 0:256]
        dtot[1] = grads[8:16, 256:512]

        @pl.when(off_diagonal)
        def _():
            gradient_copy().start()

        @pl.when(jnp.logical_not(off_diagonal))
        def _():
            dng[...] = dtot[c]

    stores = [
        pltpu.make_async_copy(src, dst, store_sem.at[i])
        for i, (src, dst) in enumerate(
            [(upg, upg_out), (dng, dng_out), (newimp, newimp_out), (proj, proj_out)]
        )
    ]

    def importance():
        @pl.when(off_diagonal)
        def _():
            gradient_copy().wait_recv()

        stores[0].start()
        stores[1].start()
        highest = lax.Precision.HIGHEST
        own_down = down[...]
        estimate = dot(dng[...], up[...].astype(jnp.float32), ((0,), (0,)), highest)
        estimate = estimate + dot(own_down.astype(jnp.float32), upg[...], ((0,), (0,)), highest)
        merged = W[y, zh, c].astype(jnp.float32) + adapter_scale * dot(own_down, up[...], ((0,), (0,)))
        newimp[...] = decay_rate * imp[...] + (1.0 - decay_rate) * jnp.abs(merged * estimate)
        stores[2].start()

    def products(stage):
        for u in range(4):
            here = 0
            for j in range(4):
                here = here + jnp.where(unit[j] == wunit[u], j, 0)

            @pl.when(jnp.maximum(here, u) == stage)
            def _(u=u):
                @pl.loop(0, 4)
                def _(i):
                    weights = W[i, wunit[u]].reshape(512, 512)
                    for r in range(2):
                        chunk = pl.ds(r * 256, 256)
                        acc[chunk] += dot(T[i, wunit[u], chunk], weights, ((1,), (0,)))

    recv_z(1, 0)
    sum_low()
    recv_z(1, 1)
    send_wz(0)
    forward_x(0, 0)
    forward_x(0, 1)
    forward_y(0, 0)
    forward_y(0, 1)
    recv_z(2, 0)
    recv_z(2, 1)
    send_wz(1)
    factor_terms()
    forward_x(1, 0)
    forward_x(1, 1)
    sum_cores()
    rest_y(0)
    far_y(0)
    recv_z(3, 0)
    recv_z(3, 1)
    forward_wz(0)
    forward_wz(1)
    forward_x(2, 0)
    forward_x(2, 1)
    sum_y()
    rest_x(0)
    far_x(0)
    recv_c(0)
    rest_wz()
    forward_y(1, 0)
    forward_y(2, 1)
    rest_x(1)
    far_x(1)
    forward_x(3, 0)
    forward_x(3, 1)
    far_wz()
    sum_gradients()
    forward_y(1, 1)
    forward_y(2, 0)
    forward_y(3, 0)
    forward_y(3, 1)
    rest_y(1)
    rest_y(2)
    importance()
    far_y(1)
    far_y(2)
    rest_x(2)
    far_x(2)
    recv_c(1)
    recv_c(2)
    rest_y(3)
    far_y(3)
    recv_c(3)
    products(0)
    products(1)
    products(2)
    rest_x(3)
    far_x(3)
    products(3)
    proj[...] = acc[...].astype(jnp.bfloat16)
    stores[3].start()

    for copy in sends:
        copy.wait_send()
    for cond, copy in z_forwards:

        @pl.when(cond)
        def _(copy=copy):
            copy.wait_send()

    @pl.when(jnp.logical_not(off_diagonal))
    def _():
        down_away.wait_send()

    @pl.when(off_diagonal)
    def _():
        for copy in down_mirror:
            copy.wait_send()
        gradient_copy().wait_send()

    for store in stores:
        store.wait()


def local(tokens, weight, down, up, cotangent, importance):
    bf16, f32 = jnp.bfloat16, jnp.float32
    dma = pltpu.SemaphoreType.DMA
    return pl.pallas_call(
        kernel,
        out_shape=(
            jax.ShapeDtypeStruct((512, 512), bf16),
            jax.ShapeDtypeStruct((8, 512), f32),
            jax.ShapeDtypeStruct((8, 256), f32),
            jax.ShapeDtypeStruct((256, 512), f32),
        ),
        in_specs=[
            pl.BlockSpec(memory_space=pltpu.VMEM if i in (2, 3) else pltpu.HBM) for i in range(6)
        ],
        out_specs=[pl.BlockSpec(memory_space=pl.ANY)] * 4,
        scratch_shapes=[
            pltpu.VMEM((4, 4, 512, 512), bf16),
            pltpu.VMEM((4, 4, 2, 256, 512), bf16),
            pltpu.VMEM((512, 512), f32),
            pltpu.VMEM((512, 512), bf16),
            pltpu.VMEM((512, 512), bf16),
            pltpu.VMEM((256, 512), f32),
            pltpu.VMEM((256, 512), f32),
            pltpu.VMEM((8, 512), f32),
            pltpu.VMEM((8, 256), f32),
            pltpu.VMEM((2, 8, 256), f32),
            pltpu.VMEM((3, 8, 256), f32),
            pltpu.VMEM((4, 16, 512), f32),
            pltpu.VMEM((4, 16, 512), f32),
            pltpu.VMEM((2, 16, 512), f32),
            pltpu.VMEM((4, 16, 512), f32),
            pltpu.VMEM((4, 16, 512), f32),
            dma((4,)), dma((4,)),
            dma((2, 4, 2)), dma((2, 4, 2)), dma((2, 4)), dma((2, 4)), dma((2, 4, 2)), dma((4, 2)),
            dma((2, 2)), dma((2, 2)), dma((2,)), dma((2,)),
            dma((2, 4, 2)), dma((2, 4, 2)), dma((2, 4)), dma((2, 4)), dma((4, 4)), dma((4, 4)),
            dma((3,)), dma((4,)), dma((3,)), dma((4,)), dma((1,)), dma((2,)),
            dma((3,)), dma((4,)), dma((3,)), dma((4,)),
            dma((3,)), dma((2,)), dma, dma,
        ],
        compiler_params=pltpu.CompilerParams(
            collective_id=0, has_side_effects=True, vmem_limit_bytes=63 * 2**20
        ),
    )(tokens, weight, down, up, cotangent, importance)


def solution(mesh):
    placed = (
        P("fsdp", "tp"),
        P("fsdp", "tp"),
        P(None, "fsdp"),
        P(None, "tp"),
        P("fsdp", "tp"),
        P("fsdp", "tp"),
    )
    return jax.shard_map(
        local,
        mesh=mesh,
        in_specs=placed,
        out_specs=(P("fsdp", "tp"), P(None, "tp"), P(None, "fsdp"), P("fsdp", "tp")),
        check_vma=False,
    )
```

time: 142 us -> 125 us (0.88)
  Pallas kernels: 132 us -> 120 us
  local copies, waits for them, and re-layouts: 8.24 us -> 4.03 us
    pallas_call x1, Pallas kernels: 132 us -> 120 us  [local(): pl.pallas_call(kernel, out_shape=(jax.ShapeDtypeStruct((512, 512), bf16),...]
    unnamed x16 -> x10, local copies, waits for them, and re-layouts: 8.24 us -> 4.03 us
where the time goes in v2:
time: 125 us; the launch traced here: 124 us
  Pallas kernels  120 us (96%)
  local copies, waits for them, and re-layouts  4.03 us (3%)
    pallas_call x1, Pallas kernels, local(): pl.pallas_call(kernel, out_shape=(jax.ShapeDtypeStruct((512, 512), bf16),...  120 us
    unnamed x10, local copies, waits for them, and re-layouts  4.03 us

profile of v2, /device:TPU:1, one launch (start us, length us, event | category | flops | bytes accessed | tf_op | source)
XLA Modules:
  0.0 124.3 jit_solution(3841062384871650966)
XLA Ops:
  0.6 119.6 %shard_map.93 = (bf16[512,512]{1,0:T(8,128)(2,1)}, f32[8,512]{1,0:T(8,128)}, f32[8,256]{1,0:T(8,128)}, f32[256,512]{1,0:T(8,128)}) custom-call(bf16[512,512]{1,0:T(8,128)(2,1)} %tok_in.1, bf16[256,512]{1,0:T(8,128)(2,1)} %w_in.1, bf16[8,256]{1,0:T(8,128)(2,1)} %down.1, bf16[8,512]{1,0:T(8,128)(2,1)} %up.1, bf16[512,512]{1,0:T(8,128)(2,1)} %cot_in.1, ...), custom_call_target="tpu_custom_call" | custom-call | tf_op jit(solution)/shard_map/pallas_call | solution.py:425
  120.2 0.0 copy-start.1
  120.2 0.0 copy-start
  120.2 1.9 %copy.14 = bf16[512,512]{1,0:T(8,128)(2,1)} copy(bf16[512,512]{1,0:T(8,128)(2,1)} %get-tuple-element.8) | data formatting | bytes 1048576
  122.2 0.0 copy-done.1
  122.2 0.0 copy-start.2
  122.2 0.6 copy.15
  122.8 0.1 copy-done.2
  122.9 0.6 copy.16
  123.5 0.0 copy-done
  123.5 0.8 copy.17
Async XLA Ops:
  120.2 1.9 %copy-start.1 = (f32[8,512]{1,0:T(8,128)S(1)}, f32[8,512]{1,0:T(8,128)}, u32[]{:S(2)}) copy-start(f32[8,512]{1,0:T(8,128)} %get-tuple-element.9) | copy-start | bytes 49156
  120.2 3.2 %copy-start = (f32[256,512]{1,0:T(8,128)S(1)}, f32[256,512]{1,0:T(8,128)}, u32[]{:S(2)}) copy-start(f32[256,512]{1,0:T(8,128)} %get-tuple-element.11) | copy-start | bytes 1572868
  122.2 0.7 copy-start.2

commit v3 on v2

--- a/solution.py
+++ b/solution.py
@@ -93,6 +93,10 @@
         sends.append(copy)
         return copy
 
+    def go_later(copy):
+        sends.append(copy)
+        return copy
+
     down_away = remote(dtot.at[2], down_t.at[c], dt_s.at[0], dt_r.at[c], sibling)
     down_mirror = [
         remote(dtot.at[2], down_t.at[c], dt_s.at[1 + core], dt_r.at[c], mirror(core)) for core in (0, 1)
@@ -116,29 +120,25 @@
     ]
     wunit = [zh, ring(zh, -1), ring(zh, 1), ring(zh, 2)]
 
-    half, quarter = 256, 128
-
-    def rows(h, size):
-        return pl.ds(h * size, size)
+    def rows(p, size):
+        return pl.ds(p * size, size)
 
     def recv(dst, sem):
         remote(dst, dst, sem, sem, sibling).wait_recv()
 
-    def send_x(j, h):
-        block = T.at[x, unit[j], rows(h, half)]
-        for side, to in enumerate((x_next, x_prev)):
-            go(remote(block, block, tx_s.at[side, j, h], tx_r.at[side, j, h], to))
-
-    def send_x0(k):
-        for side, to in enumerate((x_next, x_prev)):
-            h = k if side == 0 else 1 - k
-            block = T.at[x, zl, rows(h, half)]
-            go(remote(block, block, tx_s.at[side, 0, h], tx_r.at[side, 0, h], to))
+    tp, wp = 128, 64
+
+    def send_x(j, p, sides=(0, 1)):
+        block = T.at[x, unit[j], rows(p, tp)]
+        for side in sides:
+            to = (x_next, x_prev)[side]
+            go(remote(block, block, tx_s.at[side, j, p], tx_r.at[side, j, p], to))
 
     z_forwards = []
-
-    def send_z(j, h):
-        block = T.at[x, unit[j], rows(h, half)]
+    z_last = []
+
+    def send_z(j, p):
+        block = T.at[x, unit[j], rows(p, tp)]
         if j == 0:
             cases = ((zl < 3, l_next, 0), (zl > 0, l_prev, 1))
         else:
@@ -147,88 +147,136 @@
                 (jnp.logical_and(unit[j] > zl, zl > 0), l_prev, 1),
             )
         for cond, to, side in cases:
-            copy = remote(block, block, tz_s.at[side, j, h], tz_r.at[unit[j], h], to)
+            copy = remote(block, block, tz_s.at[side, j, p], tz_r.at[unit[j], p], to)
             z_forwards.append((cond, copy))
 
             @pl.when(cond)
             def _(copy=copy):
                 copy.start()
 
-    def recv_z(j, h):
-        recv(T.at[x, unit[j], rows(h, half)], tz_r.at[unit[j], h])
-        send_z(j, h)
-        send_x(j, h)
-
-    def forward_x(j, h):
-        near, to = (ring(x, -1), x_next) if h == 0 else (ring(x, 1), x_prev)
-        block = T.at[near, unit[j], rows(h, half)]
-        recv(block, tx_r.at[h, j, h])
-        go(remote(block, block, txh_s.at[h, j], txh_r.at[h, j], to))
+    def recv_z(j, p):
+        recv(T.at[x, unit[j], rows(p, tp)], tz_r.at[unit[j], p])
+        send_z(j, p)
+        send_x(j, p)
+
+    middle = jnp.logical_and(zl > 0, zl < 3)
+    last_x = {}
+
+    def recv_z_last(p, here):
+        block = T.at[x, unit[3], rows(p, tp)]
+        first = p not in last_x
+        if first:
+            last_x[p] = [
+                go_later(remote(block, block, tx_s.at[side, 3, p], tx_r.at[side, 3, p], to))
+                for side, to in enumerate((x_next, x_prev))
+            ]
+            for cond, to, side in (
+                (jnp.logical_and(unit[3] < zl, zl < 3), l_next, 0),
+                (jnp.logical_and(unit[3] > zl, zl > 0), l_prev, 1),
+            ):
+                copy = remote(block, block, tz_s.at[side, 3, p], tz_r.at[unit[3], p], to)
+                z_forwards.append((cond, copy))
+                z_last.append((p, cond, copy))
+
+        @pl.when(here)
+        def _():
+            recv(block, tz_r.at[unit[3], p])
+            for q, cond, copy in z_last:
+                if q == p and first:
+                    pl.when(cond)(copy.start)
+            for copy in last_x[p]:
+                copy.start()
+
+    def forward_x(j, p):
+        side = p // 2
+        near, to = (ring(x, -1), x_next) if side == 0 else (ring(x, 1), x_prev)
+        block = T.at[near, unit[j], rows(p, tp)]
+        recv(block, tx_r.at[side, j, p])
+        go(remote(block, block, txh_s.at[j, p], txh_r.at[j, p], to))
 
     def rest_x(j):
-        recv(T.at[ring(x, -1), unit[j], rows(1, half)], tx_r.at[0, j, 1])
-        recv(T.at[ring(x, 1), unit[j], rows(0, half)], tx_r.at[1, j, 0])
+        for p in (2, 3):
+            recv(T.at[ring(x, -1), unit[j], rows(p, tp)], tx_r.at[0, j, p])
+        for p in (0, 1):
+            recv(T.at[ring(x, 1), unit[j], rows(p, tp)], tx_r.at[1, j, p])
 
     def far_x(j):
-        for h in (0, 1):
-            recv(T.at[ring(x, 2), unit[j], rows(h, half)], txh_r.at[h, j])
-
-    def send_c(u, r):
-        block = W.at[ring(y, r), wunit[u], c]
-        go(remote(block, block, wc_s.at[u, r % 4], wc_r.at[u, r % 4], sibling))
-
-    def send_y(u, h):
-        block = W.at[y, wunit[u], c, rows(h, quarter)]
-        for side, to in enumerate((y_next, y_prev)):
-            go(remote(block, block, wy_s.at[side, u, h], wy_r.at[side, u, h], to))
-
-    def forward_y(u, h):
-        near, to = (ring(y, -1), y_next) if h == 0 else (ring(y, 1), y_prev)
-        block = W.at[near, wunit[u], c, rows(h, quarter)]
-        recv(block, wy_r.at[h, u, h])
-        go(remote(block, block, wyh_s.at[h, u], wyh_r.at[h, u], to))
-
-    def rest_y(u):
-        recv(W.at[ring(y, -1), wunit[u], c, rows(1, quarter)], wy_r.at[0, u, 1])
-        send_c(u, -1)
-        recv(W.at[ring(y, 1), wunit[u], c, rows(0, quarter)], wy_r.at[1, u, 0])
-        send_c(u, 1)
-
-    def far_y(u):
-        for h in (0, 1):
-            recv(W.at[ring(y, 2), wunit[u], c, rows(h, quarter)], wyh_r.at[h, u])
-        send_c(u, 2)
+        for p in range(4):
+            recv(T.at[ring(x, 2), unit[j], rows(p, tp)], txh_r.at[j, p])
+
+    def core_parts(u):
+        return (pl.ds(0, 128), pl.ds(128, 128)) if u == 3 else (pl.ds(0, 256),)
+
+    def send_c(u, r, part=0):
+        block = W.at[ring(y, r), wunit[u], c, core_parts(u)[part]]
+        go(remote(block, block, wc_s.at[u, r % 4, part], wc_r.at[u, r % 4, part], sibling))
 
     def recv_c(u):
         for r in range(4):
-            recv(W.at[ring(y, r), wunit[u], 1 - c], wc_r.at[u, r])
+            for part, where in enumerate(core_parts(u)):
+                recv(W.at[ring(y, r), wunit[u], 1 - c, where], wc_r.at[u, r, part])
+
+    def send_y(u, p, sides=(0, 1)):
+        block = W.at[y, wunit[u], c, rows(p, wp)]
+        for side in sides:
+            to = (y_next, y_prev)[side]
+            go(remote(block, block, wy_s.at[side, u, p], wy_r.at[side, u, p], to))
+
+    def forward_y(u, p):
+        side = p // 2
+        near, to = (ring(y, -1), y_next) if side == 0 else (ring(y, 1), y_prev)
+        block = W.at[near, wunit[u], c, rows(p, wp)]
+        recv(block, wy_r.at[side, u, p])
+        go(remote(block, block, wyh_s.at[u, p], wyh_r.at[u, p], to))
+        if u == 3 and p % 2 == 1:
+            send_c(u, -1 if side == 0 else 1, side)
+
+    def rest_y(u):
+        for p in (2, 3):
+            recv(W.at[ring(y, -1), wunit[u], c, rows(p, wp)], wy_r.at[0, u, p])
+        send_c(u, -1, len(core_parts(u)) - 1)
+        for p in (0, 1):
+            recv(W.at[ring(y, 1), wunit[u], c, rows(p, wp)], wy_r.at[1, u, p])
+        send_c(u, 1)
+
+    def far_y(u):
+        for p in range(4):
+            recv(W.at[ring(y, 2), wunit[u], c, rows(p, wp)], wyh_r.at[u, p])
+            if u == 3 and p == 1:
+                send_c(u, 2)
+        send_c(u, 2, len(core_parts(u)) - 1)
 
     def send_wz(k):
-        for side, to in enumerate((h_next, h_prev)):
-            h = k if side == 0 else 1 - k
-            block = W.at[y, zh, c, rows(h, quarter)]
-            go(remote(block, block, wz_s.at[side, h], wz_r.at[side, h], to))
-
-    def forward_wz(h):
-        near, to = (wunit[1], h_next) if h == 0 else (wunit[2], h_prev)
-        block = W.at[y, near, c, rows(h, quarter)]
-        recv(block, wz_r.at[h, h])
-        go(remote(block, block, wzh_s.at[h], wzh_r.at[h], to))
-        send_y(1 + h, h)
-
-    def rest_wz():
-        recv(W.at[y, wunit[1], c, rows(1, quarter)], wz_r.at[0, 1])
-        send_y(1, 1)
-        send_c(1, 0)
-        recv(W.at[y, wunit[2], c, rows(0, quarter)], wz_r.at[1, 0])
-        send_y(2, 0)
-        send_c(2, 0)
-
-    def far_wz():
-        for h in (0, 1):
-            recv(W.at[y, wunit[3], c, rows(h, quarter)], wzh_r.at[h])
-            send_y(3, h)
-        send_c(3, 0)
+        for q in (0, 1):
+            for side, to in enumerate((h_next, h_prev)):
+                p = 2 * (k if side == 0 else 1 - k) + q
+                block = W.at[y, zh, c, rows(p, wp)]
+                go(remote(block, block, wz_s.at[side, p], wz_r.at[side, p], to))
+
+    def forward_wz(p):
+        side = p // 2
+        near, to = (wunit[1], h_next) if side == 0 else (wunit[2], h_prev)
+        block = W.at[y, near, c, rows(p, wp)]
+        recv(block, wz_r.at[side, p])
+        go(remote(block, block, wzh_s.at[p], wzh_r.at[p], to))
+        send_y(1 + side, p)
+
+    def rest_wz(p):
+        u = 1 if p >= 2 else 2
+        recv(W.at[y, wunit[u], c, rows(p, wp)], wz_r.at[u - 1, p])
+        send_y(u, p)
+        if p % 2 == 1:
+            send_c(u, 0)
+
+    def far_wz(p):
+        recv(W.at[y, wunit[3], c, rows(p, wp)], wzh_r.at[p])
+        send_y(3, p, (p // 2,))
+        if p % 2 == 1:
+            send_c(3, 0, p // 2)
+
+    def far_wz_back():
+        for p in (0, 2, 1, 3):
+            send_y(3, p, (1 - p // 2,))
 
     def sum_send(buf, me, s, r, to):
         for d in range(1, len(to) + 1):
@@ -243,10 +291,17 @@
             total = total + buf[i]
         return total
 
-    send_x0(0)
-    for h in (0, 1):
-        send_z(0, h)
-        send_y(0, h)
+    for p in (0, 1):
+        send_x(0, p, (0,))
+        send_x(0, 2 + p, (1,))
+    for p in (0, 2, 1, 3):
+        send_z(0, p)
+    for p in (0, 1):
+        send_y(0, p, (0,))
+        send_y(0, 2 + p, (1,))
+    for p in (0, 1):
+        send_y(0, 2 + p, (0,))
+        send_y(0, p, (1,))
     send_c(0, 0)
     for load in loads[2:]:
         load.wait()
@@ -260,7 +315,9 @@
     arx[x, 0:8] = dot(down_columns, T[x, zl], ((1,), (1,)))
     arx[x, 8:16] = dot(up[...], cot[...], ((1,), (1,)))
     sum_send(arx, x, arx_s, arx_r, [dev(x=ring(x, d)) for d in (1, 2, 3)])
-    send_x0(1)
+    for p in (0, 1):
+        send_x(0, 2 + p, (0,))
+        send_x(0, p, (1,))
 
     def sum_low():
         arz[zl] = sum_recv(arx, x, arx_r, 4)
@@ -321,79 +378,99 @@
         newimp[...] = decay_rate * imp[...] + (1.0 - decay_rate) * jnp.abs(merged * estimate)
         stores[2].start()
 
-    def products(stage):
-        for u in range(4):
-            here = 0
-            for j in range(4):
-                here = here + jnp.where(unit[j] == wunit[u], j, 0)
-
-            @pl.when(jnp.maximum(here, u) == stage)
-            def _(u=u):
-                @pl.loop(0, 4)
-                def _(i):
-                    weights = W[i, wunit[u]].reshape(512, 512)
-                    for r in range(2):
-                        chunk = pl.ds(r * 256, 256)
-                        acc[chunk] += dot(T[i, wunit[u], chunk], weights, ((1,), (0,)))
+    def product(u, j):
+        @pl.when(unit[j] == wunit[u])
+        def _():
+            @pl.loop(0, 4)
+            def _(i):
+                weights = W[i, wunit[u]].reshape(512, 512)
+                for r in range(2):
+                    chunk = pl.ds(r * 256, 256)
+                    acc[chunk] += dot(T[i, wunit[u], chunk], weights, ((1,), (0,)))
 
     recv_z(1, 0)
     sum_low()
+    recv_z(1, 2)
     recv_z(1, 1)
+    recv_z(1, 3)
+    for p in (0, 2, 1, 3):
+            forward_x(0, p)
+    for p in (0, 2, 1, 3):
+            recv_z(2, p)
     send_wz(0)
-    forward_x(0, 0)
-    forward_x(0, 1)
-    forward_y(0, 0)
-    forward_y(0, 1)
-    recv_z(2, 0)
-    recv_z(2, 1)
+    for p in (0, 2):
+            recv_z_last(p, middle)
     send_wz(1)
+    for p in (0, 2, 1, 3):
+            forward_y(0, p)
     factor_terms()
-    forward_x(1, 0)
-    forward_x(1, 1)
+    for p in (0, 2, 1, 3):
+            forward_x(1, p)
     sum_cores()
     rest_y(0)
     far_y(0)
-    recv_z(3, 0)
-    recv_z(3, 1)
-    forward_wz(0)
-    forward_wz(1)
-    forward_x(2, 0)
-    forward_x(2, 1)
-    sum_y()
     rest_x(0)
     far_x(0)
     recv_c(0)
-    rest_wz()
-    forward_y(1, 0)
-    forward_y(2, 1)
+    product(0, 0)
+    for p in (0, 2, 1, 3):
+            forward_wz(p)
+    for p in (1, 3):
+            recv_z_last(p, middle)
+    for p in (0, 2, 1, 3):
+            forward_x(2, p)
+    for p in (0, 2):
+            recv_z_last(p, jnp.logical_not(middle))
+    sum_y()
+    for p in (0, 2, 1, 3):
+            rest_wz(p)
+    for u, p in ((1, 0), (2, 2), (1, 1), (2, 3)):
+            forward_y(u, p)
     rest_x(1)
     far_x(1)
-    forward_x(3, 0)
-    forward_x(3, 1)
-    far_wz()
-    sum_gradients()
-    forward_y(1, 1)
-    forward_y(2, 0)
-    forward_y(3, 0)
-    forward_y(3, 1)
+    product(0, 1)
+    for p in (0, 2):
+            forward_x(3, p)
+    for u, p in ((1, 2), (2, 0), (1, 3), (2, 1)):
+            forward_y(u, p)
     rest_y(1)
     rest_y(2)
-    importance()
+    for p in (1, 3):
+            recv_z_last(p, jnp.logical_not(middle))
+    for p in (0, 2, 1, 3):
+            far_wz(p)
+    far_wz_back()
+    sum_gradients()
     far_y(1)
     far_y(2)
     rest_x(2)
     far_x(2)
+    product(0, 2)
     recv_c(1)
-    recv_c(2)
+    product(1, 0)
+    for p in (0, 2, 1, 3):
+            forward_y(3, p)
+    for p in (1, 3):
+            forward_x(3, p)
+    product(1, 1)
+    product(1, 2)
+    importance()
     rest_y(3)
     far_y(3)
-    recv_c(3)
-    products(0)
-    products(1)
-    products(2)
+    recv_c(2)
+    product(2, 0)
+    product(2, 1)
+    product(2, 2)
     rest_x(3)
     far_x(3)
-    products(3)
+    product(0, 3)
+    product(1, 3)
+    product(2, 3)
+    recv_c(3)
+    product(3, 0)
+    product(3, 1)
+    product(3, 2)
+    product(3, 3)
     proj[...] = acc[...].astype(jnp.bfloat16)
     stores[3].start()
 
@@ -452,9 +529,9 @@
             pltpu.VMEM((4, 16, 512), f32),
             pltpu.VMEM((4, 16, 512), f32),
             dma((4,)), dma((4,)),
-            dma((2, 4, 2)), dma((2, 4, 2)), dma((2, 4)), dma((2, 4)), dma((2, 4, 2)), dma((4, 2)),
-            dma((2, 2)), dma((2, 2)), dma((2,)), dma((2,)),
-            dma((2, 4, 2)), dma((2, 4, 2)), dma((2, 4)), dma((2, 4)), dma((4, 4)), dma((4, 4)),
+            dma((2, 4, 4)), dma((2, 4, 4)), dma((4, 4)), dma((4, 4)), dma((2, 4, 4)), dma((4, 4)),
+            dma((2, 4)), dma((2, 4)), dma((4,)), dma((4,)),
+            dma((2, 4, 4)), dma((2, 4, 4)), dma((4, 4)), dma((4, 4)), dma((4, 4, 2)), dma((4, 4, 2)),
             dma((3,)), dma((4,)), dma((3,)), dma((4,)), dma((1,)), dma((2,)),
             dma((3,)), dma((4,)), dma((3,)), dma((4,)),
             dma((3,)), dma((2,)), dma, dma,

time: 125 us -> 116 us (0.928)
  Pallas kernels: 120 us -> 111 us
    pallas_call x1, Pallas kernels: 120 us -> 111 us  [local(): pl.pallas_call(kernel, out_shape=(jax.ShapeDtypeStruct((512, 512), bf16),...]
where the time goes in v3:
time: 116 us
  Pallas kernels  111 us (96%)
  local copies, waits for them, and re-layouts  4.03 us (3%)
    pallas_call x1, Pallas kernels, local(): pl.pallas_call(kernel, out_shape=(jax.ShapeDtypeStruct((512, 512), bf16),...  111 us
    unnamed x10, local copies, waits for them, and re-layouts  4.03 us

profile of v3, /device:TPU:1, one launch (start us, length us, event | category | flops | bytes accessed | tf_op | source)
XLA Modules:
  0.0 115.5 jit_solution(7854393666384426153)
XLA Ops:
  0.6 110.8 %shard_map.93 = (bf16[512,512]{1,0:T(8,128)(2,1)}, f32[8,512]{1,0:T(8,128)}, f32[8,256]{1,0:T(8,128)}, f32[256,512]{1,0:T(8,128)}) custom-call(bf16[512,512]{1,0:T(8,128)(2,1)} %tok_in.1, bf16[256,512]{1,0:T(8,128)(2,1)} %w_in.1, bf16[8,256]{1,0:T(8,128)(2,1)} %down.1, bf16[8,512]{1,0:T(8,128)(2,1)} %up.1, bf16[512,512]{1,0:T(8,128)(2,1)} %cot_in.1, ...), custom_call_target="tpu_custom_call" | custom-call | tf_op jit(solution)/shard_map/pallas_call | solution.py:502
  111.5 0.0 copy-start.1
  111.5 0.0 copy-start
  111.5 1.9 %copy.14 = bf16[512,512]{1,0:T(8,128)(2,1)} copy(bf16[512,512]{1,0:T(8,128)(2,1)} %get-tuple-element.8) | data formatting | bytes 1048576
  113.4 0.0 copy-done.1
  113.4 0.0 copy-start.2
  113.4 0.6 copy.15
  114.0 0.1 copy-done.2
  114.1 0.6 copy.16
  114.7 0.0 copy-done
  114.7 0.8 copy.17
Async XLA Ops:
  111.5 1.9 %copy-start.1 = (f32[8,512]{1,0:T(8,128)S(1)}, f32[8,512]{1,0:T(8,128)}, u32[]{:S(2)}) copy-start(f32[8,512]{1,0:T(8,128)} %get-tuple-element.9) | copy-start | bytes 49156
  111.5 3.2 %copy-start = (f32[256,512]{1,0:T(8,128)S(1)}, f32[256,512]{1,0:T(8,128)}, u32[]{:S(2)}) copy-start(f32[256,512]{1,0:T(8,128)} %get-tuple-element.11) | copy-start | bytes 1572868
  113.4 0.7 copy-start.2

commit v4 on v3

--- a/solution.py
+++ b/solution.py
@@ -381,12 +381,14 @@
     def product(u, j):
         @pl.when(unit[j] == wunit[u])
         def _():
-            @pl.loop(0, 4)
-            def _(i):
-                weights = W[i, wunit[u]].reshape(512, 512)
-                for r in range(2):
-                    chunk = pl.ds(r * 256, 256)
-                    acc[chunk] += dot(T[i, wunit[u], chunk], weights, ((1,), (0,)))
+            @pl.loop(0, 2)
+            def _(r):
+                chunk = pl.ds(pl.multiple_of(r * 256, 256), 256)
+                total = acc[chunk]
+                for i in range(4):
+                    weights = W[i, wunit[u]].reshape(512, 512)
+                    total = total + dot(T[i, wunit[u], chunk], weights, ((1,), (0,)))
+                acc[chunk] = total
 
     recv_z(1, 0)
     sum_low()
@@ -455,12 +457,12 @@
     product(1, 1)
     product(1, 2)
     importance()
-    rest_y(3)
-    far_y(3)
     recv_c(2)
     product(2, 0)
     product(2, 1)
     product(2, 2)
+    rest_y(3)
+    far_y(3)
     rest_x(3)
     far_x(3)
     product(0, 3)

time: 116 us -> 115 us (level)
  no operation moved by 1% of the time
where the time goes in v4:
time: 115 us
  Pallas kernels  110 us (96%)
  local copies, waits for them, and re-layouts  4.03 us (4%)
    pallas_call x1, Pallas kernels, local(): pl.pallas_call(kernel, out_shape=(jax.ShapeDtypeStruct((512, 512), bf16),...  110 us
    unnamed x10, local copies, waits for them, and re-layouts  4.03 us

profile of v4, /device:TPU:1, one launch (start us, length us, event | category | flops | bytes accessed | tf_op | source)
XLA Modules:
  0.0 114.6 jit_solution(6929308380981594391)
XLA Ops:
  0.6 109.9 %shard_map.93 = (bf16[512,512]{1,0:T(8,128)(2,1)}, f32[8,512]{1,0:T(8,128)}, f32[8,256]{1,0:T(8,128)}, f32[256,512]{1,0:T(8,128)}) custom-call(bf16[512,512]{1,0:T(8,128)(2,1)} %tok_in.1, bf16[256,512]{1,0:T(8,128)(2,1)} %w_in.1, bf16[8,256]{1,0:T(8,128)(2,1)} %down.1, bf16[8,512]{1,0:T(8,128)(2,1)} %up.1, bf16[512,512]{1,0:T(8,128)(2,1)} %cot_in.1, ...), custom_call_target="tpu_custom_call" | custom-call | tf_op jit(solution)/shard_map/pallas_call | solution.py:504
  110.5 0.0 copy-start.1
  110.5 0.0 copy-start
  110.6 1.9 %copy.14 = bf16[512,512]{1,0:T(8,128)(2,1)} copy(bf16[512,512]{1,0:T(8,128)(2,1)} %get-tuple-element.8) | data formatting | bytes 1048576
  112.5 0.0 copy-done.1
  112.5 0.0 copy-start.2
  112.5 0.6 copy.15
  113.1 0.1 copy-done.2
  113.2 0.6 copy.16
  113.8 0.0 copy-done
  113.8 0.8 copy.17
Async XLA Ops:
  110.5 1.9 %copy-start.1 = (f32[8,512]{1,0:T(8,128)S(1)}, f32[8,512]{1,0:T(8,128)}, u32[]{:S(2)}) copy-start(f32[8,512]{1,0:T(8,128)} %get-tuple-element.9) | copy-start | bytes 49156
  110.5 3.2 %copy-start = (f32[256,512]{1,0:T(8,128)S(1)}, f32[256,512]{1,0:T(8,128)}, u32[]{:S(2)}) copy-start(f32[256,512]{1,0:T(8,128)} %get-tuple-element.11) | copy-start | bytes 1572868
  112.5 0.7 copy-start.2
